TPU v7x, 128 devices: a whole 4x4x4 slice. The times are simulated.
128 devices in a mesh: grp: 4 (over y_lo, core), dev: 32 (over x, z, y_hi).
Axes of the slice: x: 4, y: 4 (y_hi: 2, y_lo: 2; y = y_hi * 2 + y_lo), z: 4, core: 2. Of those that a mesh axis runs over, the one named last changes fastest.
Arguments:
- tokens: bfloat16 [16384, 2048], P(('grp', 'dev')), may hold values from -6 to 6
- cotangent: bfloat16 [16384, 2048], P(('grp', 'dev')), may hold values from -1.5 to 1.5
- route_weight: float32 [16384, 2], P(('grp', 'dev')), may hold values from 0.1 to 1
- slot_expert: int32 [128], replicated, may hold values from 0 to 15, as said below
- targets: int32 [16384, 2], P(('grp', 'dev')), may hold values from 0 to 127, as said below
- proj_in: float32 [16, 2048, 2048], P('grp', 'dev'), may hold values from -0.125 to 0.125
- first_in: float32 [16, 2048, 2048], P('grp', 'dev'), may hold values from -6 to 6
- second_in: float32 [16, 2048, 2048], P('grp', 'dev'), may hold values from 0.01 to 1
- proj_out: float32 [16, 1024, 2048], P('grp', 'dev'), may hold values from -0.1875 to 0.1875
- first_out: float32 [16, 1024, 2048], P('grp', 'dev'), may hold values from -6 to 6
- second_out: float32 [16, 1024, 2048], P('grp', 'dev'), may hold values from 0.01 to 1
Outputs:
- mixed: bfloat16 [16384, 2048], P(('grp', 'dev'))
- token_grad: bfloat16 [16384, 2048], P(('grp', 'dev'))
- mix_grad: float32 [16384, 2], P(('grp', 'dev'))
- trained_in: float32 [16, 2048, 2048], P('grp', 'dev')
- mean_in: float32 [16, 2048, 2048], P('grp', 'dev')
- square_in: float32 [16, 2048, 2048], P('grp', 'dev')
- trained_out: float32 [16, 1024, 2048], P('grp', 'dev')
- mean_out: float32 [16, 1024, 2048], P('grp', 'dev')
- square_out: float32 [16, 1024, 2048], P('grp', 'dev')
Inputs may be any that keep to these rules, and one draw needn't show every extreme that they name: `slot_expert`: entry s is the expert held by slot s, the device s in grp+dev order; each of the 16 experts is held by at least one slot. `targets`: entry [t, k] is the slot that serves the k-th expert of token t; the two slots of a token hold different experts.
All inputs are finite; a program needn't handle non-finite values.
Results may differ from a plain program's by a relative error of at most 0.015.
The roundings to bfloat16 on the way count: a program that leaves them out, or rounds other values in their place, can miss the bound.
Values may be sent and summed in bfloat16 or wider, within the bound.
No kernel may reach another device: no remote copies, remote signals or barrier semaphores. Data moves between devices by JAX's collectives and lax.ppermute only.
A program may use at most 128 MiB of HBM per device.

v0:
```python
import jax
import jax.numpy as jnp
from jax import lax
from jax.sharding import PartitionSpec as P

D = 2048
FF = 1024
E = 16
beta_first = 0.9
beta_second = 0.95
learn_rate = 0.01
decay_rate = 0.1
adam_eps = 1e-08
bias_first = 1.0 - 0.9**10
bias_second = 1.0 - 0.95**10


def silu_parts(values):
    logistic = jax.nn.sigmoid(values)
    return (values * logistic, logistic * (1.0 + values * (1.0 - logistic)))


def slot_pass(rows_x, rows_dy, weight_up, weight_down):
    gate_up = jnp.dot(rows_x, weight_up, preferred_element_type=jnp.float32)
    gating = gate_up[:, :FF]
    upward = gate_up[:, FF:]
    active, derivative = silu_parts(gating)
    hidden = (active * upward).astype(jnp.bfloat16)
    result = jnp.dot(hidden, weight_down, preferred_element_type=jnp.float32).astype(jnp.bfloat16)
    dhidden = lax.dot_general(
        rows_dy, weight_down, (((1,), (1,)), ((), ())), preferred_element_type=jnp.float32
    )
    grad_gateup = jnp.concatenate([dhidden * upward * derivative, dhidden * active], axis=1).astype(
        jnp.bfloat16
    )
    rows_dx = lax.dot_general(
        grad_gateup, weight_up, (((1,), (1,)), ((), ())), preferred_element_type=jnp.float32
    ).astype(jnp.bfloat16)
    grad_up = lax.dot_general(
        rows_x, grad_gateup, (((0,), (0,)), ((), ())), preferred_element_type=jnp.float32
    ).astype(jnp.bfloat16)
    grad_down = lax.dot_general(
        hidden, rows_dy, (((0,), (0,)), ((), ())), preferred_element_type=jnp.float32
    ).astype(jnp.bfloat16)
    return (result, rows_dx, grad_up, grad_down)


def adam_step(weight, moment, square, gradient):
    new_moment = beta_first * moment + (1.0 - beta_first) * gradient
    new_square = beta_second * square + (1.0 - beta_second) * gradient * gradient
    update = (
        new_moment / bias_first / (jnp.sqrt(new_square / bias_second) + adam_eps)
        + decay_rate * weight
    )
    return (weight - learn_rate * update, new_moment, new_square)


def to_slots(payload_x, payload_dy):
    moved_x, moved_dy = (
        lax.all_to_all(payload_x, ("grp", "dev"), split_axis=0, concat_axis=0, tiled=True),
        lax.all_to_all(payload_dy, ("grp", "dev"), split_axis=0, concat_axis=0, tiled=True),
    )
    return (moved_x, moved_dy)


def to_sources(payload_out, payload_dx):
    moved_out, moved_dx = (
        lax.all_to_all(payload_out, ("grp", "dev"), split_axis=0, concat_axis=0, tiled=True),
        lax.all_to_all(payload_dx, ("grp", "dev"), split_axis=0, concat_axis=0, tiled=True),
    )
    return (moved_out, moved_dx)


def on_device(
    tokens,
    cotangent,
    route_weight,
    slot_expert,
    targets,
    proj_in,
    first_in,
    second_in,
    proj_out,
    first_out,
    second_out,
):
    groups = lax.axis_size("grp")
    members = lax.axis_size("dev")
    slot_count = groups * members
    tok_count = tokens.shape[0]
    assigns = 2 * tok_count
    capacity = 3 * tok_count // slot_count
    buffer_rows = slot_count * capacity
    flat_target = targets.reshape(-1)
    onehot = (flat_target[:, None] == jnp.arange(slot_count, dtype=jnp.int32)[None, :]).astype(
        jnp.int32
    )
    earlier = jnp.cumsum(onehot, axis=0) - onehot
    position = jnp.sum(earlier * onehot, axis=1)
    within = position < capacity
    dest_row = jnp.where(within, flat_target * capacity + position, buffer_rows)
    matched = dest_row[:, None] == jnp.arange(buffer_rows, dtype=jnp.int32)[None, :]
    filled = jnp.any(matched, axis=0)
    source_id = jnp.sum(
        jnp.where(matched, jnp.arange(assigns, dtype=jnp.int32)[:, None], 0), axis=0
    )
    scaled = (
        route_weight.reshape(-1)[:, None] * jnp.repeat(cotangent, 2, axis=0).astype(jnp.float32)
    ).astype(jnp.bfloat16)
    send_x = jnp.where(filled[:, None], tokens[source_id // 2], jnp.zeros((), jnp.bfloat16))
    send_dy = jnp.where(filled[:, None], scaled[source_id], jnp.zeros((), jnp.bfloat16))
    slot_x, slot_dy = to_slots(
        send_x.reshape(slot_count, capacity, D), send_dy.reshape(slot_count, capacity, D)
    )
    slot_x = slot_x.reshape(buffer_rows, D)
    slot_dy = slot_dy.reshape(buffer_rows, D)
    my_group = lax.axis_index("grp")
    group_expert = lax.dynamic_slice_in_dim(slot_expert, my_group * members, members)
    low_in = proj_in.astype(jnp.bfloat16)
    low_out = proj_out.astype(jnp.bfloat16)
    all_up, all_down = (
        lax.all_gather(low_in, "grp", axis=0, tiled=True),
        lax.all_gather(low_out, "grp", axis=0, tiled=True),
    )
    send_up = jnp.take(all_up, group_expert, axis=0)
    send_down = jnp.take(all_down, group_expert, axis=0)
    got_up, got_down = (
        lax.all_to_all(send_up, "dev", split_axis=0, concat_axis=0, tiled=True),
        lax.all_to_all(send_down, "dev", split_axis=0, concat_axis=0, tiled=True),
    )
    slot_up = got_up.reshape(D, 2 * FF)
    slot_down = got_down.reshape(FF, D)
    result, rows_dx, grad_up, grad_down = slot_pass(slot_x, slot_dy, slot_up, slot_down)
    back_out, back_dx = to_sources(
        result.reshape(slot_count, capacity, D), rows_dx.reshape(slot_count, capacity, D)
    )
    flat_out = back_out.reshape(buffer_rows, D)
    flat_dx = back_dx.reshape(buffer_rows, D)
    pick_row = jnp.where(within, flat_target * capacity + position, 0)
    assigned_out = jnp.where(
        within[:, None], flat_out[pick_row], jnp.zeros((), jnp.bfloat16)
    ).reshape(tok_count, 2, D)
    assigned_dx = jnp.where(
        within[:, None], flat_dx[pick_row], jnp.zeros((), jnp.bfloat16)
    ).reshape(tok_count, 2, D)
    out_float = assigned_out.astype(jnp.float32)
    mixed = (
        route_weight[:, 0:1] * out_float[:, 0] + route_weight[:, 1:2] * out_float[:, 1]
    ).astype(jnp.bfloat16)
    token_grad = (
        assigned_dx[:, 0].astype(jnp.float32) + assigned_dx[:, 1].astype(jnp.float32)
    ).astype(jnp.bfloat16)
    mix_grad = jnp.sum(cotangent.astype(jnp.float32)[:, None, :] * out_float, axis=2)
    rows_up, rows_down = (
        lax.all_to_all(
            grad_up.reshape(members, D // members, 2 * FF),
            "dev",
            split_axis=0,
            concat_axis=0,
            tiled=True,
        ),
        lax.all_to_all(
            grad_down.reshape(members, FF // members, D),
            "dev",
            split_axis=0,
            concat_axis=0,
            tiled=True,
        ),
    )
    holder = (group_expert[None, :] == jnp.arange(E, dtype=jnp.int32)[:, None]).astype(jnp.bfloat16)
    part_up = jnp.einsum("ed,drc->erc", holder, rows_up, preferred_element_type=jnp.float32)
    part_down = jnp.einsum("ed,drc->erc", holder, rows_down, preferred_element_type=jnp.float32)
    sum_up, sum_down = (
        lax.psum_scatter(
            part_up.astype(jnp.bfloat16), "grp", scatter_dimension=0, tiled=True
        ).astype(jnp.float32),
        lax.psum_scatter(
            part_down.astype(jnp.bfloat16), "grp", scatter_dimension=0, tiled=True
        ).astype(jnp.float32),
    )
    trained_in, mean_in, square_in = adam_step(proj_in, first_in, second_in, sum_up)
    trained_out, mean_out, square_out = adam_step(proj_out, first_out, second_out, sum_down)
    return (
        mixed,
        token_grad,
        mix_grad,
        trained_in,
        mean_in,
        square_in,
        trained_out,
        mean_out,
        square_out,
    )


def solution(mesh):
    in_specs = (
        P(("grp", "dev"), None),
        P(("grp", "dev"), None),
        P(("grp", "dev"), None),
        P(),
        P(("grp", "dev"), None),
        P("grp", "dev", None),
        P("grp", "dev", None),
        P("grp", "dev", None),
        P("grp", "dev", None),
        P("grp", "dev", None),
        P("grp", "dev", None),
    )
    out_specs = (
        P(("grp", "dev"), None),
        P(("grp", "dev"), None),
        P(("grp", "dev"), None),
        P("grp", "dev", None),
        P("grp", "dev", None),
        P("grp", "dev", None),
        P("grp", "dev", None),
        P("grp", "dev", None),
        P("grp", "dev", None),
    )
    return jax.shard_map(
        on_device, mesh=mesh, in_specs=in_specs, out_specs=out_specs, check_vma=False
    )
```

profile of v0, /device:TPU:1, one launch (start us, length us, event | category | flops | bytes accessed | tf_op | source)
XLA Modules:
  0.0 679.6 jit_solution(7755972250965304729)
XLA Ops:
  27.5 5.2 gather.29
  36.9 44.3 %all_to_all.40 = bf16[128,3,2048]{2,1,0:T(4,128)(2,1)S(1)} all-to-all(bf16[128,3,2048]{2,1,0:T(4,128)(2,1)S(1)} %get-tuple-element.59), channel_id=1, replica_groups=mesh['grp'=4,'dev'=32] {'grp','dev'}, dimensions={0} | all-to-all | bytes 3145728 | tf_op jit(solution)/shard_map/all_to_all | solution.py:60
  81.3 7.1 %all-to-all-start.4 = ((bf16[128,3,2048]{2,1,0:T(4,128)(2,1)}), bf16[128,3,2048]{2,1,0:T(4,128)(2,1)}, u32[]{:S(2)}, u32[]{:S(2)}) async-start(bf16[128,3,2048]{2,1,0:T(4,128)(2,1)} %get-tuple-element.58), calls=%async_computation.4 | async-start | bytes 4194304 | tf_op jit(solution)/shard_map/all_to_all | solution.py:61
  88.5 7.2 %gather_fusion.1 = bf16[32,64,2048]{2,1,0:T(8,128)(2,1)} fusion(bf16[16,64,2048]{2,1,0:T(8,128)(2,1)} %all-gather.3.cloned.1.call-done, s32[1024]{0:T(1024)S(1)} %pad_clamp_fusion.2), kind=kCustom, calls=%fused_computation.1 | custom fusion | bytes 16777344 | tf_op jit(solution)/shard_map/jit(_take)/gather | solution.py:125
  95.7 7.5 %broadcast_select_fusion = bf16[32,64,2048]{2,1,0:T(8,128)(2,1)} fusion(bf16[32,64,2048]{2,1,0:T(8,128)(2,1)} %gather_fusion.1, pred[32]{0:T(512)(128)(4,1)S(1)} %get-tuple-element.53), kind=kLoop, calls=%fused_computation.8 | loop fusion | flops 4194304 | bytes 16777248 | tf_op jit(solution)/shard_map/jit(_take)/select_n | solution.py:125
  103.2 15.1 %all-to-all-done.4 = bf16[128,3,2048]{2,1,0:T(4,128)(2,1)} async-done(((bf16[128,3,2048]{2,1,0:T(4,128)(2,1)}), bf16[128,3,2048]{2,1,0:T(4,128)(2,1)}, u32[]{:S(2)}, u32[]{:S(2)}) %all-to-all-start.4) | async-done | bytes 1572896 | tf_op jit(solution)/shard_map/all_to_all | solution.py:61
  118.2 5.0 all-to-all-start.1
  125.3 106.8 %all-gather.5.cloned.1.call-done = bf16[16,32,2048]{2,1,0:T(8,128)(2,1)} async-done(((bf16[4,32,2048]{2,1,0:T(8,128)(2,1)}), bf16[16,32,2048]{2,1,0:T(8,128)(2,1)}) %all-gather.5.cloned.1.call-update) | async-done | bytes 2097168 | tf_op jit(solution)/shard_map/all_gather | solution.py:123
  236.5 4.6 broadcast_select_fusion.1
  241.2 7.3 %all-to-all-done.1 = bf16[32,64,2048]{2,1,0:T(8,128)(2,1)} async-done(((bf16[32,64,2048]{2,1,0:T(8,128)(2,1)}), bf16[32,64,2048]{2,1,0:T(8,128)(2,1)}, u32[]{:S(2)}, u32[]{:S(2)}) %all-to-all-start.1) | async-done | bytes 8388640 | tf_op jit(solution)/shard_map/all_to_all | solution.py:128
  248.4 13.3 %all-to-all-start.2 = ((bf16[32,32,2048]{2,1,0:T(8,128)(2,1)}), bf16[32,32,2048]{2,1,0:T(8,128)(2,1)}, u32[]{:S(2)}, u32[]{:S(2)}) async-start(bf16[32,32,2048]{2,1,0:T(8,128)(2,1)} %broadcast_select_fusion.1), calls=%async_computation.2 | async-start | bytes 8388608 | tf_op jit(solution)/shard_map/all_to_all | solution.py:129
  264.2 5.2 reshape.242
  269.3 8.5 %fusion.40 = f32[384,2048]{1,0:T(8,128)} fusion(bf16[384,2048]{1,0:T(8,128)(2,1)S(1)} %copy-done.5, bf16[2048,2048]{1,0:T(8,128)(2,1)} %bitcast.4), kind=kOutput, calls=%fused_computation.89 | convolution fusion | flops 3221225472 | bytes 13107200 | tf_op jit(solution)/shard_map/dot_general | solution.py:24
  277.8 38.0 %all-to-all-done.2 = bf16[32,32,2048]{2,1,0:T(8,128)(2,1)} async-done(((bf16[32,32,2048]{2,1,0:T(8,128)(2,1)}), bf16[32,32,2048]{2,1,0:T(8,128)(2,1)}, u32[]{:S(2)}, u32[]{:S(2)}) %all-to-all-start.2) | async-done | bytes 4194336 | tf_op jit(solution)/shard_map/all_to_all | solution.py:129
  315.9 7.2 %multiply_convert_fusion.2 = (bf16[384,1024]{1,0:T(8,128)(2,1)}, bf16[384,1024]{1,0:T(8,128)(2,1)}, bf16[384,1024]{1,0:T(8,128)(2,1)S(1)}) fusion(f32[384,2048]{1,0:T(8,128)} %fusion.40, bf16[384,2048]{1,0:T(8,128)(2,1)} %reshape.242, bf16[1024,2048]{1,0:T(8,128)(2,1)} %bitcast.5), kind=kOutput, calls=%fused_computation.30 | convolution fusion | flops 1616510976 | bytes 11272192 | tf_op jit(solution)/shard_map/dot_general | solution.py:30
  327.4 8.8 %all-to-all-start.7 = ((bf16[32,32,2048]{2,1,0:T(8,128)(2,1)}), bf16[32,32,2048]{2,1,0:T(8,128)(2,1)}, u32[]{:S(2)}, u32[]{:S(2)}) async-start(bf16[32,32,2048]{2,1,0:T(8,128)(2,1)} %bitcast.54), calls=%async_computation.8 | async-start | bytes 8388608 | tf_op jit(solution)/shard_map/all_to_all | solution.py:162
  336.2 8.1 %convolution_convert_fusion = bf16[2048,2048]{1,0:T(8,128)(2,1)} fusion(bf16[384,2048]{1,0:T(8,128)(2,1)S(1)} %copy-done.5, bf16[384,1024]{1,0:T(8,128)(2,1)} %get-tuple-element.56, bf16[384,1024]{1,0:T(8,128)(2,1)} %get-tuple-element.55), kind=kOutput, calls=%fused_computation.9 | convolution fusion | flops 3228565504 | bytes 11534336 | tf_op jit(solution)/shard_map/dot_general | solution.py:39
  344.3 45.0 %all-to-all-done.7 = bf16[32,32,2048]{2,1,0:T(8,128)(2,1)} async-done(((bf16[32,32,2048]{2,1,0:T(8,128)(2,1)}), bf16[32,32,2048]{2,1,0:T(8,128)(2,1)}, u32[]{:S(2)}, u32[]{:S(2)}) %all-to-all-start.7) | async-done | bytes 4194336 | tf_op jit(solution)/shard_map/all_to_all | solution.py:162
  389.3 9.3 %all-to-all-start.6 = ((bf16[32,64,2048]{2,1,0:T(8,128)(2,1)}), bf16[32,64,2048]{2,1,0:T(8,128)(2,1)}, u32[]{:S(2)}, u32[]{:S(2)}) async-start(bf16[32,64,2048]{2,1,0:T(8,128)(2,1)} %bitcast.53), calls=%async_computation.6 | async-start | bytes 16777216 | tf_op jit(solution)/shard_map/all_to_all | solution.py:155
  398.7 6.8 fusion.7
  408.0 8.8 %reduce-scatter.3.cloned.1.call-start = ((), (), s32[]{:S(2)}) async-start(), calls=%async_computation.12 | async-start | bytes 5242880 | tf_op jit(solution)/shard_map/reduce_scatter | solution.py:174
  416.8 103.2 %all-to-all-done.6 = bf16[32,64,2048]{2,1,0:T(8,128)(2,1)} async-done(((bf16[32,64,2048]{2,1,0:T(8,128)(2,1)}), bf16[32,64,2048]{2,1,0:T(8,128)(2,1)}, u32[]{:S(2)}, u32[]{:S(2)}) %all-to-all-start.6) | async-done | bytes 8388640 | tf_op jit(solution)/shard_map/all_to_all | solution.py:155
  520.0 12.5 %fusion.4 = bf16[16,64,2048]{2,0,1:T(8,128)(2,1)S(1)} fusion(bf16[32,64,2048]{2,1,0:T(8,128)(2,1)} %all-to-all-done.6, s32[32]{0:T(128)S(1)} %get-tuple-element.54), kind=kOutput, calls=%fused_computation.14 | convolution fusion | flops 136315392 | bytes 12583040 | tf_op jit(solution)/shard_map/ed,drc->erc/dot_general | solution.py:171
  536.8 7.5 %convolution_convert_fusion.2 = bf16[384,2048]{1,0:T(8,128)(2,1)S(1)} fusion(bf16[2048,2048]{1,0:T(8,128)(2,1)} %bitcast.4, bf16[384,1024]{1,0:T(8,128)(2,1)} %get-tuple-element.56, bf16[384,1024]{1,0:T(8,128)(2,1)} %get-tuple-element.55), kind=kOutput, calls=%fused_computation.17 | convolution fusion | flops 3225157632 | bytes 11534336 | tf_op jit(solution)/shard_map/dot_general | solution.py:36
  546.7 24.6 %all-to-all-start.5 = ((bf16[128,3,2048]{2,1,0:T(4,128)(2,1)}), bf16[128,3,2048]{2,1,0:T(4,128)(2,1)S(1)}, u32[]{:S(2)}, u32[]{:S(2)}) async-start(bf16[128,3,2048]{2,1,0:T(4,128)(2,1)} %reshape.243), calls=%async_computation.5 | async-start | bytes 4194304 | tf_op jit(solution)/shard_map/all_to_all | solution.py:69
  571.2 5.4 convolution_convert_fusion.3
  576.7 5.2 reshape.240
  581.8 22.4 %all-to-all-done.5 = bf16[128,3,2048]{2,1,0:T(4,128)(2,1)S(1)} async-done(((bf16[128,3,2048]{2,1,0:T(4,128)(2,1)}), bf16[128,3,2048]{2,1,0:T(4,128)(2,1)S(1)}, u32[]{:S(2)}, u32[]{:S(2)}) %all-to-all-start.5) | async-done | bytes 1572896 | tf_op jit(solution)/shard_map/all_to_all | solution.py:69
  605.5 7.5 %all-to-all-start.3 = ((bf16[128,3,2048]{2,1,0:T(4,128)(2,1)}), bf16[128,3,2048]{2,1,0:T(4,128)(2,1)}, u32[]{:S(2)}, u32[]{:S(2)}) async-start(bf16[128,3,2048]{2,1,0:T(4,128)(2,1)} %reshape.240), calls=%async_computation.3 | async-start | bytes 4194304 | tf_op jit(solution)/shard_map/all_to_all | solution.py:68
  620.4 25.2 %all-to-all-done.3 = bf16[128,3,2048]{2,1,0:T(4,128)(2,1)} async-done(((bf16[128,3,2048]{2,1,0:T(4,128)(2,1)}), bf16[128,3,2048]{2,1,0:T(4,128)(2,1)}, u32[]{:S(2)}, u32[]{:S(2)}) %all-to-all-start.3) | async-done | bytes 1572896 | tf_op jit(solution)/shard_map/all_to_all | solution.py:68
  661.7 4.4 multiply_subtract_fusion.1
  666.1 6.5 multiply_subtract_fusion
  (93 shorter events, 71.8 us)
Async XLA Ops:
  7.2 17.2 %copy-start = (bf16[128,2048]{1,0:T(8,128)(2,1)S(1)}, bf16[128,2048]{1,0:T(8,128)(2,1)}, u32[]{:S(2)}) copy-start(bf16[128,2048]{1,0:T(8,128)(2,1)} %param.11) | copy-start | bytes 1572868
  7.2 2.9 copy-start.8
  7.2 3.3 copy-start.7
  7.2 81.3 %all-gather.3.cloned.1.call-start = ((), (), s32[]{:S(2)}) async-start(), calls=%async_computation.10 | async-start | bytes 5242880 | tf_op jit(solution)/shard_map/all_gather | solution.py:122
  11.5 2.5 copy-start.9
  81.3 7.1 %copy-start.10 = (s32[128]{0:T(128)S(1)}, s32[128]{0:T(128)}, u32[]{:S(2)}) copy-start(s32[128]{0:T(128)} %param.14) | copy-start | bytes 1540
  81.3 37.0 %all-to-all-start.4 = ((bf16[128,3,2048]{2,1,0:T(4,128)(2,1)}), bf16[128,3,2048]{2,1,0:T(4,128)(2,1)}, u32[]{:S(2)}, u32[]{:S(2)}) async-start(bf16[128,3,2048]{2,1,0:T(4,128)(2,1)} %get-tuple-element.58), calls=%async_computation.4 | async-start | bytes 4194304 | tf_op jit(solution)/shard_map/all_to_all | solution.py:61
  118.2 130.2 %all-to-all-start.1 = ((bf16[32,64,2048]{2,1,0:T(8,128)(2,1)}), bf16[32,64,2048]{2,1,0:T(8,128)(2,1)}, u32[]{:S(2)}, u32[]{:S(2)}) async-start(bf16[32,64,2048]{2,1,0:T(8,128)(2,1)} %broadcast_select_fusion), calls=%async_computation.1 | async-start | bytes 16777216 | tf_op jit(solution)/shard_map/all_to_all | solution.py:128
  123.2 109.0 %all-gather.5.cloned.1.call-start = ((), (), s32[]{:S(2)}) async-start(), calls=%async_computation.11 | async-start | bytes 2621440 | tf_op jit(solution)/shard_map/all_gather | solution.py:123
  248.4 67.5 %all-to-all-start.2 = ((bf16[32,32,2048]{2,1,0:T(8,128)(2,1)}), bf16[32,32,2048]{2,1,0:T(8,128)(2,1)}, u32[]{:S(2)}, u32[]{:S(2)}) async-start(bf16[32,32,2048]{2,1,0:T(8,128)(2,1)} %broadcast_select_fusion.1), calls=%async_computation.2 | async-start | bytes 8388608 | tf_op jit(solution)/shard_map/all_to_all | solution.py:129
  264.2 5.2 copy-start.5
  315.9 7.2 %copy-start.6 = (bf16[384,2048]{1,0:T(8,128)(2,1)S(1)}, bf16[384,2048]{1,0:T(8,128)(2,1)}, u32[]{:S(2)}) copy-start(bf16[384,2048]{1,0:T(8,128)(2,1)} %reshape.242) | copy-start | bytes 4718596
  323.0 4.4 copy-start.11
  327.4 61.9 %all-to-all-start.7 = ((bf16[32,32,2048]{2,1,0:T(8,128)(2,1)}), bf16[32,32,2048]{2,1,0:T(8,128)(2,1)}, u32[]{:S(2)}, u32[]{:S(2)}) async-start(bf16[32,32,2048]{2,1,0:T(8,128)(2,1)} %bitcast.54), calls=%async_computation.8 | async-start | bytes 8388608 | tf_op jit(solution)/shard_map/all_to_all | solution.py:162
  389.3 130.7 %all-to-all-start.6 = ((bf16[32,64,2048]{2,1,0:T(8,128)(2,1)}), bf16[32,64,2048]{2,1,0:T(8,128)(2,1)}, u32[]{:S(2)}, u32[]{:S(2)}) async-start(bf16[32,64,2048]{2,1,0:T(8,128)(2,1)} %bitcast.53), calls=%async_computation.6 | async-start | bytes 16777216 | tf_op jit(solution)/shard_map/all_to_all | solution.py:155
  398.7 263.0 %reduce-scatter.5.cloned.1.call-start = ((), (), s32[]{:S(2)}) async-start(), calls=%async_computation.13 | async-start | bytes 2621440 | tf_op jit(solution)/shard_map/reduce_scatter | solution.py:177
  408.0 258.0 %reduce-scatter.3.cloned.1.call-start = ((), (), s32[]{:S(2)}) async-start(), calls=%async_computation.12 | async-start | bytes 5242880 | tf_op jit(solution)/shard_map/reduce_scatter | solution.py:174
  546.7 57.5 %all-to-all-start.5 = ((bf16[128,3,2048]{2,1,0:T(4,128)(2,1)}), bf16[128,3,2048]{2,1,0:T(4,128)(2,1)S(1)}, u32[]{:S(2)}, u32[]{:S(2)}) async-start(bf16[128,3,2048]{2,1,0:T(4,128)(2,1)} %reshape.243), calls=%async_computation.5 | async-start | bytes 4194304 | tf_op jit(solution)/shard_map/all_to_all | solution.py:69
  604.2 1.3 copy-start.3
  605.5 40.0 %all-to-all-start.3 = ((bf16[128,3,2048]{2,1,0:T(4,128)(2,1)}), bf16[128,3,2048]{2,1,0:T(4,128)(2,1)}, u32[]{:S(2)}, u32[]{:S(2)}) async-start(bf16[128,3,2048]{2,1,0:T(4,128)(2,1)} %reshape.240), calls=%async_computation.3 | async-start | bytes 4194304 | tf_op jit(solution)/shard_map/all_to_all | solution.py:68
  651.8 2.7 copy-start.2
  661.7 4.4 copy-start.4
  666.1 6.5 copy-start.1
Sparse Core Ops, SparseCore 0:
  10.3 72.6 all-gather.2
  126.3 105.8 all-gather.4
  408.2 106.6 reduce-scatter.4
  537.0 107.0 reduce-scatter.2
where the time goes:
time: 689 us; the launch traced here: 680 us
  waiting for transfers between devices  363 us (53%)
  starting transfers between devices  84.4 us (12%)
  local copies, waits for them, and re-layouts  71.7 us (10%)
  matrix products  60.3 us (9%)
  blocking collectives  44.3 us (6%)
  other arithmetic  41.2 us (6%)
  between operations  14.5 us (2%)
    all_gather x1, waiting for transfers between devices, on_device(): lax.all_gather(low_out, 'grp', axis=0, tiled=True)  107 us
    all_to_all x1, waiting for transfers between devices, on_device(): lax.all_to_all(grad_up.reshape(members, D // members, 2 * FF), 'dev', spl...  103 us
    all_to_all x1, waiting for transfers between devices, on_device(): lax.all_to_all(grad_down.reshape(members, FF // members, D), 'dev', split...  45 us
    all_to_all x1, blocking collectives, to_slots(): lax.all_to_all(payload_x, ('grp', 'dev'), split_axis=0, concat_axis=0, ti...  44.3 us
    all_to_all x1, waiting for transfers between devices, on_device(): lax.all_to_all(send_down, 'dev', split_axis=0, concat_axis=0, tiled=True)  38 us
    all_to_all x1, waiting for transfers between devices, to_sources(): lax.all_to_all(payload_out, ('grp', 'dev'), split_axis=0, concat_axis=0,...  25.2 us
    all_to_all x1, starting transfers between devices, to_sources(): lax.all_to_all(payload_dx, ('grp', 'dev'), split_axis=0, concat_axis=0, t...  24.6 us
    all_to_all x1, waiting for transfers between devices, to_sources(): lax.all_to_all(payload_dx, ('grp', 'dev'), split_axis=0, concat_axis=0, t...  22.4 us
  transfers between devices with their start and end apart: 11, of which 8 were waited for; matrix products, arithmetic and copies ran while one was open for 22% of the time, Pallas kernels for 0%

commit v1 on v0

--- a/solution.py
+++ b/solution.py
@@ -120,7 +120,9 @@
     low_out = proj_out.astype(jnp.bfloat16)
     all_up, all_down = (
         lax.all_gather(low_in, "grp", axis=0, tiled=True),
-        lax.all_gather(low_out, "grp", axis=0, tiled=True),
+        jnp.concatenate(
+            lax.all_to_all(jnp.stack([low_out] * lax.axis_size("grp")), "grp", 0, 0), axis=0
+        ),
     )
     send_up = jnp.take(all_up, group_expert, axis=0)
     send_down = jnp.take(all_down, group_expert, axis=0)

time: 689 us -> 709 us (1.029)
  waiting for transfers between devices: 363 us -> 387 us
    all_to_all x1, waiting for transfers between devices: 7.26 us -> 120 us  [on_device(): lax.all_to_all(send_up, 'dev', split_axis=0, concat_axis=0, tiled=True)]
    all_gather x1 -> x0, waiting for transfers between devices: 107 us -> none  [on_device(): lax.all_gather(low_out, 'grp', axis=0, tiled=True)]
    all_to_all x1, waiting for transfers between devices: 15.1 us -> 28.9 us  [to_slots(): lax.all_to_all(payload_dy, ('grp', 'dev'), split_axis=0, concat_axis=0, t...]
    all_to_all x0 -> x1, waiting for transfers between devices: none -> 10 us  [on_device(): lax.all_to_all(jnp.stack([low_out] * lax.axis_size('grp')), 'grp', 0, 0)]
    all_to_all x1, starting transfers between devices: 24.6 us -> 15.4 us  [to_sources(): lax.all_to_all(payload_dx, ('grp', 'dev'), split_axis=0, concat_axis=0, t...]
where the time goes in v1:
time: 709 us; the launch traced here: 699 us
  waiting for transfers between devices  387 us (55%)
  starting transfers between devices  80.5 us (11%)
  local copies, waits for them, and re-layouts  72.1 us (10%)
  matrix products  60.3 us (9%)
  blocking collectives  44.4 us (6%)
  other arithmetic  40.4 us (6%)
  between operations  14.5 us (2%)
    all_to_all x1, waiting for transfers between devices, on_device(): lax.all_to_all(send_up, 'dev', split_axis=0, concat_axis=0, tiled=True)  120 us
    all_to_all x1, waiting for transfers between devices, on_device(): lax.all_to_all(grad_up.reshape(members, D // members, 2 * FF), 'dev', spl...  99 us
    all_to_all x1, waiting for transfers between devices, on_device(): lax.all_to_all(grad_down.reshape(members, FF // members, D), 'dev', split...  45.8 us
    all_to_all x1, blocking collectives, to_slots(): lax.all_to_all(payload_x, ('grp', 'dev'), split_axis=0, concat_axis=0, ti...  44.4 us
    all_to_all x1, waiting for transfers between devices, on_device(): lax.all_to_all(send_down, 'dev', split_axis=0, concat_axis=0, tiled=True)  36.2 us
    all_to_all x1, waiting for transfers between devices, to_slots(): lax.all_to_all(payload_dy, ('grp', 'dev'), split_axis=0, concat_axis=0, t...  28.9 us
    all_to_all x1, waiting for transfers between devices, to_sources(): lax.all_to_all(payload_out, ('grp', 'dev'), split_axis=0, concat_axis=0,...  25.2 us
    all_to_all x1, waiting for transfers between devices, to_sources(): lax.all_to_all(payload_dx, ('grp', 'dev'), split_axis=0, concat_axis=0, t...  22.4 us
  transfers between devices with their start and end apart: 11, of which 8 were waited for; matrix products, arithmetic and copies ran while one was open for 22% of the time, Pallas kernels for 0%

profile of v1, /device:TPU:1, one launch (start us, length us, event | category | flops | bytes accessed | tf_op | source)
XLA Modules:
  0.0 699.4 jit_solution(12335312577771703270)
XLA Ops:
  27.5 5.2 gather.29
  36.9 44.4 %all_to_all.45 = bf16[128,3,2048]{2,1,0:T(4,128)(2,1)} all-to-all(bf16[128,3,2048]{2,1,0:T(4,128)(2,1)S(1)} %get-tuple-element.59), channel_id=1, replica_groups=mesh['grp'=4,'dev'=32] {'grp','dev'}, dimensions={0} | all-to-all | bytes 3145728 | tf_op jit(solution)/shard_map/all_to_all | solution.py:60
  81.4 6.6 all-to-all-start.5
  89.3 28.9 %all-to-all-done.5 = bf16[128,3,2048]{2,1,0:T(4,128)(2,1)S(1)} async-done(((bf16[128,3,2048]{2,1,0:T(4,128)(2,1)}), bf16[128,3,2048]{2,1,0:T(4,128)(2,1)S(1)}, u32[]{:S(2)}, u32[]{:S(2)}) %all-to-all-start.5) | async-done | bytes 1572896 | tf_op jit(solution)/shard_map/all_to_all | solution.py:61
  124.4 7.2 %gather_fusion.1 = bf16[32,64,2048]{2,1,0:T(8,128)(2,1)} fusion(bf16[16,64,2048]{2,1,0:T(8,128)(2,1)} %all-gather.2.cloned.1.call-done, s32[1024]{0:T(1024)S(1)} %pad_clamp_fusion.2), kind=kCustom, calls=%fused_computation.1 | custom fusion | bytes 16777344 | tf_op jit(solution)/shard_map/jit(_take)/gather | solution.py:127
  131.6 7.5 %broadcast_select_fusion = bf16[32,64,2048]{2,1,0:T(8,128)(2,1)} fusion(bf16[32,64,2048]{2,1,0:T(8,128)(2,1)} %gather_fusion.1, pred[32]{0:T(512)(128)(4,1)S(1)} %get-tuple-element.53), kind=kLoop, calls=%fused_computation.8 | loop fusion | flops 4194304 | bytes 16777248 | tf_op jit(solution)/shard_map/jit(_take)/select_n | solution.py:127
  139.1 10.0 %all-to-all-done.2 = bf16[4,4,32,2048]{3,2,1,0:T(8,128)(2,1)S(1)} async-done(((bf16[4,4,32,2048]{3,2,1,0:T(8,128)(2,1)}), bf16[4,4,32,2048]{3,2,1,0:T(8,128)(2,1)S(1)}, u32[]{:S(2)}, u32[]{:S(2)}) %all-to-all-start.2) | async-done | bytes 2097184 | tf_op jit(solution)/shard_map/all_to_all | solution.py:124
  149.2 5.0 all-to-all-start.1
  156.9 4.6 broadcast_select_fusion.1
  161.5 119.5 %all-to-all-done.1 = bf16[32,64,2048]{2,1,0:T(8,128)(2,1)} async-done(((bf16[32,64,2048]{2,1,0:T(8,128)(2,1)}), bf16[32,64,2048]{2,1,0:T(8,128)(2,1)}, u32[]{:S(2)}, u32[]{:S(2)}) %all-to-all-start.1) | async-done | bytes 8388640 | tf_op jit(solution)/shard_map/all_to_all | solution.py:130
  281.0 15.1 %all-to-all-start.3 = ((bf16[32,32,2048]{2,1,0:T(8,128)(2,1)}), bf16[32,32,2048]{2,1,0:T(8,128)(2,1)}, u32[]{:S(2)}, u32[]{:S(2)}) async-start(bf16[32,32,2048]{2,1,0:T(8,128)(2,1)} %broadcast_select_fusion.1), calls=%async_computation.3 | async-start | bytes 8388608 | tf_op jit(solution)/shard_map/all_to_all | solution.py:131
  298.7 5.2 reshape.248
  303.9 8.5 %fusion.40 = f32[384,2048]{1,0:T(8,128)} fusion(bf16[384,2048]{1,0:T(8,128)(2,1)S(1)} %copy-done.7, bf16[2048,2048]{1,0:T(8,128)(2,1)} %bitcast.4), kind=kOutput, calls=%fused_computation.89 | convolution fusion | flops 3221225472 | bytes 13107200 | tf_op jit(solution)/shard_map/dot_general | solution.py:24
  312.3 36.2 %all-to-all-done.3 = bf16[32,32,2048]{2,1,0:T(8,128)(2,1)} async-done(((bf16[32,32,2048]{2,1,0:T(8,128)(2,1)}), bf16[32,32,2048]{2,1,0:T(8,128)(2,1)}, u32[]{:S(2)}, u32[]{:S(2)}) %all-to-all-start.3) | async-done | bytes 4194336 | tf_op jit(solution)/shard_map/all_to_all | solution.py:131
  348.6 7.2 %multiply_convert_fusion.2 = (bf16[384,1024]{1,0:T(8,128)(2,1)}, bf16[384,1024]{1,0:T(8,128)(2,1)}, bf16[384,1024]{1,0:T(8,128)(2,1)S(1)}) fusion(f32[384,2048]{1,0:T(8,128)} %fusion.40, bf16[384,2048]{1,0:T(8,128)(2,1)} %reshape.248, bf16[1024,2048]{1,0:T(8,128)(2,1)} %bitcast.6), kind=kOutput, calls=%fused_computation.30 | convolution fusion | flops 1616510976 | bytes 11272192 | tf_op jit(solution)/shard_map/dot_general | solution.py:30
  360.1 9.7 %all-to-all-start.8 = ((bf16[32,32,2048]{2,1,0:T(8,128)(2,1)}), bf16[32,32,2048]{2,1,0:T(8,128)(2,1)}, u32[]{:S(2)}, u32[]{:S(2)}) async-start(bf16[32,32,2048]{2,1,0:T(8,128)(2,1)} %bitcast.56), calls=%async_computation.9 | async-start | bytes 8388608 | tf_op jit(solution)/shard_map/all_to_all | solution.py:164
  369.8 8.1 %convolution_convert_fusion = bf16[2048,2048]{1,0:T(8,128)(2,1)} fusion(bf16[384,2048]{1,0:T(8,128)(2,1)S(1)} %copy-done.7, bf16[384,1024]{1,0:T(8,128)(2,1)} %get-tuple-element.56, bf16[384,1024]{1,0:T(8,128)(2,1)} %get-tuple-element.55), kind=kOutput, calls=%fused_computation.9 | convolution fusion | flops 3228565504 | bytes 11534336 | tf_op jit(solution)/shard_map/dot_general | solution.py:39
  377.9 45.8 %all-to-all-done.8 = bf16[32,32,2048]{2,1,0:T(8,128)(2,1)} async-done(((bf16[32,32,2048]{2,1,0:T(8,128)(2,1)}), bf16[32,32,2048]{2,1,0:T(8,128)(2,1)}, u32[]{:S(2)}, u32[]{:S(2)}) %all-to-all-start.8) | async-done | bytes 4194336 | tf_op jit(solution)/shard_map/all_to_all | solution.py:164
  423.8 8.2 %all-to-all-start.7 = ((bf16[32,64,2048]{2,1,0:T(8,128)(2,1)}), bf16[32,64,2048]{2,1,0:T(8,128)(2,1)}, u32[]{:S(2)}, u32[]{:S(2)}) async-start(bf16[32,64,2048]{2,1,0:T(8,128)(2,1)} %bitcast.55), calls=%async_computation.7 | async-start | bytes 16777216 | tf_op jit(solution)/shard_map/all_to_all | solution.py:157
  432.0 6.8 fusion.7
  441.3 8.8 %reduce-scatter.3.cloned.1.call-start = ((), (), s32[]{:S(2)}) async-start(), calls=%async_computation.12 | async-start | bytes 5242880 | tf_op jit(solution)/shard_map/reduce_scatter | solution.py:176
  450.1 99.0 %all-to-all-done.7 = bf16[32,64,2048]{2,1,0:T(8,128)(2,1)} async-done(((bf16[32,64,2048]{2,1,0:T(8,128)(2,1)}), bf16[32,64,2048]{2,1,0:T(8,128)(2,1)}, u32[]{:S(2)}, u32[]{:S(2)}) %all-to-all-start.7) | async-done | bytes 8388640 | tf_op jit(solution)/shard_map/all_to_all | solution.py:157
  549.1 12.5 %fusion.4 = bf16[16,64,2048]{2,0,1:T(8,128)(2,1)S(1)} fusion(bf16[32,64,2048]{2,1,0:T(8,128)(2,1)} %all-to-all-done.7, s32[32]{0:T(128)S(1)} %get-tuple-element.54), kind=kOutput, calls=%fused_computation.14 | convolution fusion | flops 136315392 | bytes 12583040 | tf_op jit(solution)/shard_map/ed,drc->erc/dot_general | solution.py:173
  565.9 7.5 %convolution_convert_fusion.2 = bf16[384,2048]{1,0:T(8,128)(2,1)S(1)} fusion(bf16[2048,2048]{1,0:T(8,128)(2,1)} %bitcast.4, bf16[384,1024]{1,0:T(8,128)(2,1)} %get-tuple-element.56, bf16[384,1024]{1,0:T(8,128)(2,1)} %get-tuple-element.55), kind=kOutput, calls=%fused_computation.17 | convolution fusion | flops 3225157632 | bytes 11534336 | tf_op jit(solution)/shard_map/dot_general | solution.py:36
  575.7 15.4 %all-to-all-start.6 = ((bf16[128,3,2048]{2,1,0:T(4,128)(2,1)}), bf16[128,3,2048]{2,1,0:T(4,128)(2,1)S(1)}, u32[]{:S(2)}, u32[]{:S(2)}) async-start(bf16[128,3,2048]{2,1,0:T(4,128)(2,1)} %reshape.249), calls=%async_computation.6 | async-start | bytes 4194304 | tf_op jit(solution)/shard_map/all_to_all | solution.py:69
  591.1 5.4 convolution_convert_fusion.3
  596.5 5.2 reshape.246
  601.7 22.4 %all-to-all-done.6 = bf16[128,3,2048]{2,1,0:T(4,128)(2,1)S(1)} async-done(((bf16[128,3,2048]{2,1,0:T(4,128)(2,1)}), bf16[128,3,2048]{2,1,0:T(4,128)(2,1)S(1)}, u32[]{:S(2)}, u32[]{:S(2)}) %all-to-all-start.6) | async-done | bytes 1572896 | tf_op jit(solution)/shard_map/all_to_all | solution.py:69
  625.4 7.5 %all-to-all-start.4 = ((bf16[128,3,2048]{2,1,0:T(4,128)(2,1)}), bf16[128,3,2048]{2,1,0:T(4,128)(2,1)}, u32[]{:S(2)}, u32[]{:S(2)}) async-start(bf16[128,3,2048]{2,1,0:T(4,128)(2,1)} %reshape.246), calls=%async_computation.4 | async-start | bytes 4194304 | tf_op jit(solution)/shard_map/all_to_all | solution.py:68
  640.3 25.2 %all-to-all-done.4 = bf16[128,3,2048]{2,1,0:T(4,128)(2,1)} async-done(((bf16[128,3,2048]{2,1,0:T(4,128)(2,1)}), bf16[128,3,2048]{2,1,0:T(4,128)(2,1)}, u32[]{:S(2)}, u32[]{:S(2)}) %all-to-all-start.4) | async-done | bytes 1572896 | tf_op jit(solution)/shard_map/all_to_all | solution.py:68
  681.6 4.4 multiply_subtract_fusion.1
  685.9 6.5 multiply_subtract_fusion
  (97 shorter events, 75.4 us)
Async XLA Ops:
  7.2 17.2 %copy-start = (bf16[128,2048]{1,0:T(8,128)(2,1)S(1)}, bf16[128,2048]{1,0:T(8,128)(2,1)}, u32[]{:S(2)}) copy-start(bf16[128,2048]{1,0:T(8,128)(2,1)} %param.11) | copy-start | bytes 1572868
  7.2 2.9 copy-start.10
  7.2 3.6 copy-start.9
  7.2 117.2 %all-gather.2.cloned.1.call-start = ((), (), s32[]{:S(2)}) async-start(), calls=%async_computation.11 | async-start | bytes 5242880 | tf_op jit(solution)/shard_map/all_gather | solution.py:122
  11.9 2.5 copy-start.11
  81.4 36.8 %all-to-all-start.5 = ((bf16[128,3,2048]{2,1,0:T(4,128)(2,1)}), bf16[128,3,2048]{2,1,0:T(4,128)(2,1)S(1)}, u32[]{:S(2)}, u32[]{:S(2)}) async-start(bf16[128,3,2048]{2,1,0:T(4,128)(2,1)} %get-tuple-element.58), calls=%async_computation.5 | async-start | bytes 4194304 | tf_op jit(solution)/shard_map/all_to_all | solution.py:61
  118.2 2.0 copy-start.4
  120.0 4.3 copy-start.12
  120.2 28.9 %all-to-all-start.2 = ((bf16[4,4,32,2048]{3,2,1,0:T(8,128)(2,1)}), bf16[4,4,32,2048]{3,2,1,0:T(8,128)(2,1)S(1)}, u32[]{:S(2)}, u32[]{:S(2)}) async-start(bf16[4,4,32,2048]{3,2,1,0:T(8,128)(2,1)} %stack.2), calls=%async_computation.2 | async-start | bytes 4194304 | tf_op jit(solution)/shard_map/all_to_all | solution.py:124
  149.2 131.9 %all-to-all-start.1 = ((bf16[32,64,2048]{2,1,0:T(8,128)(2,1)}), bf16[32,64,2048]{2,1,0:T(8,128)(2,1)}, u32[]{:S(2)}, u32[]{:S(2)}) async-start(bf16[32,64,2048]{2,1,0:T(8,128)(2,1)} %broadcast_select_fusion), calls=%async_computation.1 | async-start | bytes 16777216 | tf_op jit(solution)/shard_map/all_to_all | solution.py:130
  161.5 134.7 %copy-start.3 = (bf16[128,3,2048]{2,1,0:T(4,128)(2,1)S(1)}, bf16[128,3,2048]{2,1,0:T(4,128)(2,1)}, u32[]{:S(2)}) copy-start(bf16[128,3,2048]{2,1,0:T(4,128)(2,1)} %all_to_all.45) | copy-start | bytes 4718596
  281.0 67.6 %all-to-all-start.3 = ((bf16[32,32,2048]{2,1,0:T(8,128)(2,1)}), bf16[32,32,2048]{2,1,0:T(8,128)(2,1)}, u32[]{:S(2)}, u32[]{:S(2)}) async-start(bf16[32,32,2048]{2,1,0:T(8,128)(2,1)} %broadcast_select_fusion.1), calls=%async_computation.3 | async-start | bytes 8388608 | tf_op jit(solution)/shard_map/all_to_all | solution.py:131
  298.7 5.2 copy-start.7
  348.6 7.2 %copy-start.8 = (bf16[384,2048]{1,0:T(8,128)(2,1)S(1)}, bf16[384,2048]{1,0:T(8,128)(2,1)}, u32[]{:S(2)}) copy-start(bf16[384,2048]{1,0:T(8,128)(2,1)} %reshape.248) | copy-start | bytes 4718596
  355.8 4.4 copy-start.13
  360.1 63.7 %all-to-all-start.8 = ((bf16[32,32,2048]{2,1,0:T(8,128)(2,1)}), bf16[32,32,2048]{2,1,0:T(8,128)(2,1)}, u32[]{:S(2)}, u32[]{:S(2)}) async-start(bf16[32,32,2048]{2,1,0:T(8,128)(2,1)} %bitcast.56), calls=%async_computation.9 | async-start | bytes 8388608 | tf_op jit(solution)/shard_map/all_to_all | solution.py:164
  423.8 125.3 %all-to-all-start.7 = ((bf16[32,64,2048]{2,1,0:T(8,128)(2,1)}), bf16[32,64,2048]{2,1,0:T(8,128)(2,1)}, u32[]{:S(2)}, u32[]{:S(2)}) async-start(bf16[32,64,2048]{2,1,0:T(8,128)(2,1)} %bitcast.55), calls=%async_computation.7 | async-start | bytes 16777216 | tf_op jit(solution)/shard_map/all_to_all | solution.py:157
  431.9 249.6 %reduce-scatter.5.cloned.1.call-start = ((), (), s32[]{:S(2)}) async-start(), calls=%async_computation.13 | async-start | bytes 2621440 | tf_op jit(solution)/shard_map/reduce_scatter | solution.py:179
  441.3 244.6 %reduce-scatter.3.cloned.1.call-start = ((), (), s32[]{:S(2)}) async-start(), calls=%async_computation.12 | async-start | bytes 5242880 | tf_op jit(solution)/shard_map/reduce_scatter | solution.py:176
  575.7 48.4 %all-to-all-start.6 = ((bf16[128,3,2048]{2,1,0:T(4,128)(2,1)}), bf16[128,3,2048]{2,1,0:T(4,128)(2,1)S(1)}, u32[]{:S(2)}, u32[]{:S(2)}) async-start(bf16[128,3,2048]{2,1,0:T(4,128)(2,1)} %reshape.249), calls=%async_computation.6 | async-start | bytes 4194304 | tf_op jit(solution)/shard_map/all_to_all | solution.py:69
  624.1 1.3 copy-start.5
  625.4 40.0 %all-to-all-start.4 = ((bf16[128,3,2048]{2,1,0:T(4,128)(2,1)}), bf16[128,3,2048]{2,1,0:T(4,128)(2,1)}, u32[]{:S(2)}, u32[]{:S(2)}) async-start(bf16[128,3,2048]{2,1,0:T(4,128)(2,1)} %reshape.246), calls=%async_computation.4 | async-start | bytes 4194304 | tf_op jit(solution)/shard_map/all_to_all | solution.py:68
  671.7 2.7 copy-start.2
  681.6 4.4 copy-start.6
  685.9 6.5 copy-start.1
Sparse Core Ops, SparseCore 0:
  10.3 72.6 all-gather.1
  441.4 95.6 reduce-scatter.4
  566.0 97.9 reduce-scatter.2
